TPU v7x, 32 devices: a whole 2x2x4 slice. The times are simulated.
32 devices in a mesh: parts: 2 (over y), cls: 16 (over z, x, core).
Axes of the slice: x: 2, y: 2, z: 4, core: 2. Of those that a mesh axis runs over, the one named last changes fastest.
Arguments:
- images: bfloat16 [2048, 128, 128], P(('parts', 'cls')), parts along dimension 0, may hold values from -6 to 6
- mask_radius: int32 [2048], P(('parts', 'cls')), parts along dimension 0, may hold values from 40 to 64
- rotation_prior: int32 [2048], P(('parts', 'cls')), parts along dimension 0, may hold values from 0 to 63
- candidates: int32 [2048, 8], P(('parts', 'cls')), parts along dimension 0, may hold values from 0 to 31, all different within a row; in each aligned block of 64 rows (0 to 63, 64 to 127, ...) at most 32 rows name the same one
- references: bfloat16 [64, 64, 4096], P(('parts', 'cls')), parts along dimension 0, may hold values from -0.19921875 to 0.19921875
- noise_inverse_power: float32 [2048], replicated, may hold values from 0.5 to 2
- class_bias: float32 [64], P(('parts', 'cls')), parts along dimension 0, may hold values from -1.5 to 300
Outputs:
- class_sums: float32 [64, 64, 4096], P(('parts', 'cls')), parts along dimension 0
- occupancy: float32 [64, 64], P(('parts', 'cls')), parts along dimension 0
- log_norm: float32 [2048], P(('parts', 'cls')), parts along dimension 0
There are 2 independent parts, one for each index of `parts`. A program takes and returns all parts, laid end to end along the dimension named above; an argument that names none is the same for every part. Nothing has to cross between parts.
Inputs may be any that keep to these rules, and one draw needn't show every extreme that they name: `candidates`: each row names 8 different classes. Among the rows of one device no class is named more than 32 times, a bound that some block reaches.
All inputs are finite; a program needn't handle non-finite values.
Results may differ from a plain program's by a relative error of at most 0.0097.
Values may be sent and summed in bfloat16 or wider, within the bound.
A program may use at most 128 MiB of HBM per device.

v0:
```python
import math

import jax
import jax.numpy as jnp
from jax import lax
from jax.sharding import PartitionSpec as P

BAND = 32
SIDE = 3


KAPPA = 2.0


def dft_tables(pixels, band_size):
    pixel_idx = jnp.arange(pixels, dtype=jnp.int32)
    freq_x = jnp.arange(band_size, dtype=jnp.int32)
    angles_x = (
        2.0 * math.pi / pixels * (pixel_idx[:, None] * freq_x[None, :] % pixels).astype(jnp.float32)
    )
    row_table = jnp.concatenate([jnp.cos(angles_x), -jnp.sin(angles_x)], axis=1).astype(
        jnp.bfloat16
    )
    freq_y = jnp.arange(2 * band_size, dtype=jnp.int32) - band_size
    angles_y = (
        2.0 * math.pi / pixels * (freq_y[:, None] * pixel_idx[None, :] % pixels).astype(jnp.float32)
    )
    cos_y = jnp.cos(angles_y)
    sin_y = jnp.sin(angles_y)
    upper = jnp.concatenate([cos_y, sin_y], axis=1)
    lower = jnp.concatenate([-sin_y, cos_y], axis=1)
    col_table = jnp.concatenate([upper, lower], axis=0).astype(jnp.bfloat16)
    return (row_table, col_table)


def spectra_of(images, mask_radius, row_table, col_table):
    row_count, pixels, _ = images.shape
    band_size = row_table.shape[1] // 2
    centre = jnp.arange(pixels, dtype=jnp.int32) - pixels // 2
    radius_sq = centre[:, None] * centre[:, None] + centre[None, :] * centre[None, :]
    inside = radius_sq[None, :, :] <= (mask_radius * mask_radius)[:, None, None]
    masked = jnp.where(inside, images, jnp.zeros((), jnp.bfloat16))
    partial_value = jnp.dot(
        masked.reshape(row_count * pixels, pixels), row_table, preferred_element_type=jnp.float32
    )
    partial_value = partial_value.astype(jnp.bfloat16).reshape(row_count, pixels, 2, band_size)
    partial_value = partial_value.transpose(0, 2, 1, 3).reshape(row_count, 2 * pixels, band_size)
    whole = (
        jnp.einsum("ym,pmx->pyx", col_table, partial_value, preferred_element_type=jnp.float32)
        / pixels
    )
    return whole.reshape(row_count, 4 * band_size * band_size).astype(jnp.bfloat16)


def phase_tables(pixels, band_size, side_len):
    freq_y = jnp.arange(2 * band_size, dtype=jnp.int32) - band_size
    freq_x = jnp.arange(band_size, dtype=jnp.int32)
    offsets = jnp.arange(side_len, dtype=jnp.int32) - side_len // 2
    shift_y = jnp.repeat(offsets, side_len)
    horizontal_displacement = jnp.tile(offsets, side_len)
    phase_arg = (
        freq_y[None, :, None] * shift_y[:, None, None]
        + freq_x[None, None, :] * horizontal_displacement[:, None, None]
    ) % pixels
    angles = 2.0 * math.pi / pixels * phase_arg.astype(jnp.float32).reshape(side_len * side_len, -1)
    return (jnp.cos(angles), jnp.sin(angles))


def translated_images(
    reference_block, noise_inverse_power, cosine_lookup_matrix, sine_lookup_matrix
):
    half_len = reference_block.shape[-1] // 2
    real_part = reference_block[:, :half_len].astype(jnp.float32) * noise_inverse_power[None, :]
    imag_part = reference_block[:, half_len:].astype(jnp.float32) * noise_inverse_power[None, :]
    cos_b = cosine_lookup_matrix[:, None, :]
    sin_b = sine_lookup_matrix[:, None, :]
    rot_real = real_part[None] * cos_b - imag_part[None] * sin_b
    turned_sine_term = real_part[None] * sin_b + imag_part[None] * cos_b
    stack = jnp.concatenate([rot_real, turned_sine_term], axis=-1).astype(jnp.bfloat16)
    return stack.reshape(-1, reference_block.shape[-1])


def penalty_lookup(reference_block, noise_inverse_power):
    half_len = reference_block.shape[-1] // 2
    real_part = reference_block[:, :half_len].astype(jnp.float32)
    imag_part = reference_block[:, half_len:].astype(jnp.float32)
    return 0.5 * jnp.sum(
        noise_inverse_power[None, :] * (real_part * real_part + imag_part * imag_part), axis=1
    )


def score_slots(block_spectra, centres, stack, penalty, bias_value, rot_count):
    slot_count = block_spectra.shape[0]
    cross_term = jnp.dot(block_spectra, stack.T, preferred_element_type=jnp.float32)
    cross_term = cross_term.reshape(slot_count, -1, rot_count)
    angle_step = jnp.arange(rot_count, dtype=jnp.float32)[None, :] - centres[:, None]
    prior_term = KAPPA * jnp.cos(2.0 * math.pi / rot_count * angle_step)
    total = cross_term - penalty[None, None, :] + bias_value + prior_term[:, None, :]
    return total.reshape(slot_count, -1)


def shift_back(gathered, cosine_lookup_matrix, sine_lookup_matrix):
    half_len = gathered.shape[-1] // 2
    real_block_part = gathered[..., :half_len]
    imaginary_block_part = gathered[..., half_len:]
    largest_score_seen = lax.Precision.HIGHEST
    real_running_sum = jnp.einsum(
        "iqz,iz->qz", real_block_part, cosine_lookup_matrix, precision=largest_score_seen
    ) + jnp.einsum(
        "iqz,iz->qz", imaginary_block_part, sine_lookup_matrix, precision=largest_score_seen
    )
    imaginary_running_sum = jnp.einsum(
        "iqz,iz->qz", imaginary_block_part, cosine_lookup_matrix, precision=largest_score_seen
    ) - jnp.einsum("iqz,iz->qz", real_block_part, sine_lookup_matrix, precision=largest_score_seen)
    return jnp.concatenate([real_running_sum, imaginary_running_sum], axis=-1)


def local(
    images, mask_radius, rotation_prior, candidates, references, noise_inverse_power, class_bias
):
    row_count = images.shape[0]
    classes_on_device, rot_count, freq_len = references.shape
    top_count = candidates.shape[1]
    devices = lax.axis_size("cls")
    reference_groups_list = classes_on_device * devices
    maximum_holding = max(2, 2 * row_count * top_count // reference_groups_list)
    hypotheses = SIDE * SIDE * rot_count
    row_table, col_table = dft_tables(images.shape[1], BAND)
    spectra = spectra_of(images, mask_radius, row_table, col_table)
    cosine_lookup_matrix, sine_lookup_matrix = phase_tables(images.shape[1], BAND, SIDE)
    flat_ids = candidates.reshape(-1)
    placement_coordinate = jnp.arange(row_count * top_count, dtype=jnp.int32)
    same = (flat_ids[None, :] == flat_ids[:, None]) & (
        placement_coordinate[None, :] < placement_coordinate[:, None]
    )
    earlier = jnp.sum(same.astype(jnp.int32), axis=1)
    slot_index = flat_ids * maximum_holding + earlier
    filled = (
        jnp.zeros((reference_groups_list * maximum_holding,), jnp.int32)
        .at[slot_index]
        .set(placement_coordinate + 1)
    )
    live_slot = filled > 0
    entry_index = jnp.maximum(filled - 1, 0)
    owner_row = entry_index // top_count
    outgoing = jnp.where(live_slot[:, None], spectra[owner_row], jnp.zeros((), jnp.bfloat16))
    outgoing = outgoing.reshape(devices, classes_on_device, maximum_holding, freq_len)
    centres_out = jnp.where(live_slot, rotation_prior[owner_row], 0).astype(jnp.bfloat16)
    centres_out = centres_out.reshape(devices, classes_on_device, maximum_holding)
    stacks = [
        translated_images(
            references[device_local], noise_inverse_power, cosine_lookup_matrix, sine_lookup_matrix
        )
        for device_local in range(classes_on_device)
    ]
    displacement_costs = [
        penalty_lookup(references[device_local], noise_inverse_power)
        for device_local in range(classes_on_device)
    ]
    arrived, arrived_centres = (
        lax.all_to_all(outgoing, "cls", split_axis=0, concat_axis=0, tiled=True),
        lax.all_to_all(centres_out, "cls", split_axis=0, concat_axis=0, tiled=True),
    )
    sources = arrived.shape[0]
    width = arrived.shape[2]
    blocks = []
    for score_device_local in range(classes_on_device):
        score_block_spectra = arrived[:, score_device_local].reshape(sources * width, freq_len)
        centres = (
            arrived_centres[:, score_device_local].reshape(sources * width).astype(jnp.float32)
        )
        scored = score_slots(
            score_block_spectra,
            centres,
            stacks[score_device_local],
            displacement_costs[score_device_local],
            class_bias[score_device_local],
            rot_count,
        )
        blocks.append(scored.reshape(sources, width, hypotheses))
    scores = jnp.stack(blocks, axis=1)
    returned = lax.all_to_all(scores, "cls", split_axis=0, concat_axis=0, tiled=True)
    self_class_scores = returned.reshape(reference_groups_list * maximum_holding, hypotheses)[
        slot_index
    ]
    per_particle = self_class_scores.reshape(row_count, top_count * hypotheses)
    top_peak = jnp.max(per_particle, axis=1)
    log_norm = top_peak + jnp.log(jnp.sum(jnp.exp(per_particle - top_peak[:, None]), axis=1))
    own_weights = jnp.exp(self_class_scores - jnp.repeat(log_norm, top_count)[:, None]).astype(
        jnp.bfloat16
    )
    weight_buffer = jnp.where(
        live_slot[:, None], own_weights[entry_index], jnp.zeros((), jnp.bfloat16)
    )
    weight_buffer = weight_buffer.reshape(devices, classes_on_device, maximum_holding, hypotheses)
    weights = lax.all_to_all(weight_buffer, "cls", split_axis=0, concat_axis=0, tiled=True)
    output_scale_factor = classes_on_device * rot_count / row_count
    sum_list = []
    occ_list = []
    for device_local in range(classes_on_device):
        block_weights = weights[:, device_local].reshape(-1, hypotheses)
        block_spectra = arrived[:, device_local].reshape(-1, freq_len)
        occupied = jnp.sum(
            block_weights.astype(jnp.float32).reshape(-1, SIDE * SIDE, rot_count), axis=(0, 1)
        )
        occ_list.append(occupied * output_scale_factor)
        gathered = jnp.einsum(
            "sh,sf->hf", block_weights, block_spectra, preferred_element_type=jnp.float32
        )
        gathered = gathered.reshape(SIDE * SIDE, rot_count, freq_len)
        sum_list.append(
            shift_back(gathered, cosine_lookup_matrix, sine_lookup_matrix) * output_scale_factor
        )
    return (jnp.stack(sum_list, axis=0), jnp.stack(occ_list, axis=0), log_norm)


def solution(mesh):
    in_specs = (
        P(("parts", "cls"), None, None),
        P(("parts", "cls")),
        P(("parts", "cls")),
        P(("parts", "cls"), None),
        P(("parts", "cls"), None, None),
        P(),
        P(("parts", "cls")),
    )
    out_specs = (P(("parts", "cls"), None, None), P(("parts", "cls"), None), P(("parts", "cls")))
    return jax.shard_map(local, mesh=mesh, in_specs=in_specs, out_specs=out_specs, check_vma=False)
```

profile of v0, /device:TPU:0, one launch (start us, length us, event | category | flops | bytes accessed | tf_op | source)
XLA Modules:
  0.0 431.3 jit_solution(7663020974760518753)
XLA Ops:
  10.4 2.4 scatter_custom_fusion
  12.9 40.0 %fusion.66 = bf16[1024]{0:T(1024)(128)(2,1)S(1)} fusion(s32[]{:T(128)} %bitcast.28, s32[]{:T(128)} %bitcast.29, s32[]{:T(128)} %bitcast.30, s32[]{:T(128)} %bitcast.31, s32[]{:T(128)} %bitcast.32, s32[]{:T(128)} %bitcast.33, s32[]{:T(128)} %bitcast.34, s32[]{:T(128)} %bitcast.35, s32[]{:T(128)} %bitcast.36, s32[]{:T(128)} %bitcast.37, s32[]{:T(128)} %bitcast.38, ...), kind=kLoop, calls=%fused_computation.129 | loop fusion | flops 145408 | bytes 6400 | tf_op jit(solution)/shard_map/convert_element_type | solution.py:148
  53.6 7.4 %all-to-all-start.1 = ((bf16[16,2,32]{2,1,0:T(2,128)(2,1)}), bf16[16,2,32]{2,1,0:T(2,128)(2,1)S(1)}, u32[]{:S(2)}, u32[]{:S(2)}) async-start(bf16[16,2,32]{2,1,0:T(2,128)(2,1)} %reshape.392), calls=%async_computation.1 | async-start | bytes 16384 | tf_op jit(solution)/shard_map/all_to_all | solution.py:162
  62.2 2.1 compare_select_fusion
  69.8 7.7 %gather_fusion = bf16[1024,4096]{1,0:T(8,128)(2,1)} fusion(bf16[64,4096]{1,0:T(8,128)(2,1)S(1)} %copy.54, s32[1024]{0:T(1024)S(1)} %get-tuple-element.46), kind=kCustom, calls=%fused_computation | custom fusion | bytes 16781312 | tf_op jit(solution)/shard_map/gather | solution.py:146
  77.5 7.2 %broadcast_select_fusion = bf16[16,2,32,4096]{3,2,1,0:T(8,128)(2,1)} fusion(bf16[16,2,32,4096]{3,2,1,0:T(8,128)(2,1)} %bitcast.178, pred[16,2,32]{2,1,0:T(4,128)(4,1)S(1)} %broadcast_in_dim.121), kind=kLoop, calls=%fused_computation.5 | loop fusion | flops 4194304 | bytes 16778240 | tf_op jit(solution)/shard_map/jit(_where)/select_n | solution.py:146
  84.8 6.2 %all-to-all-start = ((bf16[16,2,32,4096]{3,2,1,0:T(8,128)(2,1)}), bf16[16,2,32,4096]{3,2,1,0:T(8,128)(2,1)}, u32[]{:S(2)}, u32[]{:S(2)}) async-start(bf16[16,2,32,4096]{3,2,1,0:T(8,128)(2,1)} %broadcast_select_fusion), calls=%async_computation | async-start | bytes 16777216 | tf_op jit(solution)/shard_map/all_to_all | solution.py:161
  94.7 4.2 subtract_convert_fusion.1
  101.4 140.3 %all-to-all-done = bf16[16,2,32,4096]{3,2,1,0:T(8,128)(2,1)} async-done(((bf16[16,2,32,4096]{3,2,1,0:T(8,128)(2,1)}), bf16[16,2,32,4096]{3,2,1,0:T(8,128)(2,1)}, u32[]{:S(2)}, u32[]{:S(2)}) %all-to-all-start) | async-done | bytes 8388640 | tf_op jit(solution)/shard_map/all_to_all | solution.py:161
  241.7 5.3 %fusion.77 = (bf16[16,1,32,4096]{3,2,1,0:T(8,128)(2,1)}, bf16[16,1,32,4096]{3,2,1,0:T(8,128)(2,1)S(1)}) fusion(bf16[16,2,32,4096]{3,2,1,0:T(8,128)(2,1)} %all-to-all-done), kind=kLoop, calls=%fused_computation.157 | loop fusion | bytes 16777216 | tf_op jit(solution)/shard_map/slice | solution.py:168
  248.9 3.3 fusion.24
  252.2 2.8 reshape.522
  255.0 3.1 copy.109
  258.2 6.5 %fusion.18 = f32[512,9,64]{0,2,1:T(8,128)S(1)} fusion(bf16[512,4096,1]{1,0,2:T(8,128)(2,1)} %bitcast.183, bf16[9,64,2048]{2,1,0:T(8,128)(2,1)} %get-tuple-element.30, bf16[9,64,2048]{2,1,0:T(8,128)(2,1)} %get-tuple-element.29, f32[512,64]{0,1:T(8,128)S(1)} %copy-done.6, f32[]{:T(128)} %bitcast.27, f32[64]{0:T(128)S(1)} %copy-done.11), kind=kOutput, calls=%fused_computation.38 | convolution fusion | flops 2426241024 | bytes 10223876 | tf_op jit(solution)/shard_map/dot_general | solution.py:94
  264.7 2.8 reshape.521
  267.4 3.1 copy.108
  272.4 36.5 %all-to-all-start.2 = ((f32[16,2,32,576]{3,2,1,0:T(8,128)}), f32[16,2,32,576]{3,2,1,0:T(8,128)S(1)}, u32[]{:S(2)}, u32[]{:S(2)}) async-start(f32[16,2,32,576]{3,2,1,0:T(8,128)} %copy.57), calls=%async_computation.2 | async-start | bytes 5242880 | tf_op jit(solution)/shard_map/all_to_all | solution.py:182
  308.9 50.2 %all-to-all-done.2 = f32[16,2,32,576]{3,2,1,0:T(8,128)S(1)} async-done(((f32[16,2,32,576]{3,2,1,0:T(8,128)}), f32[16,2,32,576]{3,2,1,0:T(8,128)S(1)}, u32[]{:S(2)}, u32[]{:S(2)}) %all-to-all-start.2) | async-done | bytes 2359328 | tf_op jit(solution)/shard_map/all_to_all | solution.py:182
  359.1 2.5 gather_fusion.1
  367.1 4.0 gather_fusion.2
  371.4 44.6 %all_to_all.20 = bf16[16,2,32,576]{3,2,1,0:T(8,128)(2,1)S(1)} all-to-all(bf16[16,2,32,576]{3,2,1,0:T(8,128)(2,1)S(1)} %broadcast_select_fusion.1), channel_id=1, replica_groups=mesh['parts'=2,'cls'=16] {'cls'}, dimensions={0} | all-to-all | bytes 2359296 | tf_op jit(solution)/shard_map/all_to_all | solution.py:196
  417.1 4.6 %fusion.85 = f32[9,64,4096]{2,1,0:T(8,128)S(1)} fusion(bf16[9,64,512]{2,1,0:T(8,128)(2,1)S(1)} %bitcast.190, bf16[512,4096,1]{1,0,2:T(8,128)(2,1)} %bitcast.186), kind=kOutput, calls=%fused_computation.165 | convolution fusion | flops 2415919104 | bytes 14221312 | tf_op jit(solution)/shard_map/sh,sf->hf/dot_general | solution.py:207
  421.7 2.7 fusion.84
  425.0 4.4 %multiply_reduce_fusion.2 = (f32[2048,64]{0,1:T(8,128)S(1)}, f32[2048,64]{0,1:T(8,128)S(1)}, f32[2048,64]{0,1:T(8,128)S(1)}, f32[2048,64]{0,1:T(8,128)S(1)}, f32...) fusion(f32[9,64,4096]{2,1,0:T(8,128)S(1)} %fusion.85, ...), kind=kLoop, calls=%fused_computation.20 | loop fusion | flops 17825792 | bytes 23216128 | tf_op jit(solution)/shard_map/iqz,iz->qz/dot_general | solution.py:109
  (109 shorter events, 36.2 us)
Async XLA Ops:
  53.6 31.2 %all-to-all-start.1 = ((bf16[16,2,32]{2,1,0:T(2,128)(2,1)}), bf16[16,2,32]{2,1,0:T(2,128)(2,1)S(1)}, u32[]{:S(2)}, u32[]{:S(2)}) async-start(bf16[16,2,32]{2,1,0:T(2,128)(2,1)} %reshape.392), calls=%async_computation.1 | async-start | bytes 16384 | tf_op jit(solution)/shard_map/all_to_all | solution.py:162
  84.8 6.9 %copy-start.9 = (f32[2]{0:T(128)S(1)}, f32[2]{0:T(128)}, u32[]{:S(2)}) copy-start(f32[2]{0:T(128)} %param.13) | copy-start | bytes 28
  84.8 7.5 %copy-start.3 = (bf16[2,64,4096]{2,1,0:T(8,128)(2,1)S(1)}, bf16[2,64,4096]{2,1,0:T(8,128)(2,1)}, u32[]{:S(2)}) copy-start(bf16[2,64,4096]{2,1,0:T(8,128)(2,1)} %param.11) | copy-start | bytes 3145732
  84.8 7.6 %copy-start.8 = (f32[2048]{0:T(1024)S(1)}, f32[2048]{0:T(1024)}, u32[]{:S(2)}) copy-start(f32[2048]{0:T(1024)} %param.12) | copy-start | bytes 24580
  84.8 156.9 %all-to-all-start = ((bf16[16,2,32,4096]{3,2,1,0:T(8,128)(2,1)}), bf16[16,2,32,4096]{3,2,1,0:T(8,128)(2,1)}, u32[]{:S(2)}, u32[]{:S(2)}) async-start(bf16[16,2,32,4096]{3,2,1,0:T(8,128)(2,1)} %broadcast_select_fusion), calls=%async_computation | async-start | bytes 16777216 | tf_op jit(solution)/shard_map/all_to_all | solution.py:161
  241.7 7.3 %copy-start.2 = (bf16[9,64,2048]{2,1,0:T(8,128)(2,1)S(1)}, bf16[9,64,2048]{2,1,0:T(8,128)(2,1)}, u32[]{:S(2)}) copy-start(bf16[9,64,2048]{2,1,0:T(8,128)(2,1)} %get-tuple-element.40) | copy-start | bytes 7077892
  241.7 7.3 %copy-start.7 = (f32[512,64]{0,1:T(8,128)S(1)}, f32[512,64]{0,1:T(8,128)}, u32[]{:S(2)}) copy-start(f32[512,64]{0,1:T(8,128)} %cosine_multiply_fusion) | copy-start | bytes 393220
  241.7 7.3 %copy-start.12 = (f32[64]{0:T(128)S(1)}, f32[64]{0:T(128)}, u32[]{:S(2)}) copy-start(f32[64]{0:T(128)} %get-tuple-element.118) | copy-start | bytes 772
  247.0 2.0 copy-start.1
  255.0 3.1 copy-start.6
  255.0 3.2 copy-start.11
  272.4 86.7 %all-to-all-start.2 = ((f32[16,2,32,576]{3,2,1,0:T(8,128)}), f32[16,2,32,576]{3,2,1,0:T(8,128)S(1)}, u32[]{:S(2)}, u32[]{:S(2)}) async-start(f32[16,2,32,576]{3,2,1,0:T(8,128)} %copy.57), calls=%async_computation.2 | async-start | bytes 5242880 | tf_op jit(solution)/shard_map/all_to_all | solution.py:182
  365.4 5.8 %copy-start.10 = (f32[64]{0:T(128)}, f32[64]{0:T(128)S(1)}, u32[]{:S(2)}) copy-start(f32[64]{0:T(128)S(1)} %log_add_fusion) | copy-start | bytes 772
  417.1 4.6 %copy-start = (bf16[16,1,32,4096]{3,2,1,0:T(8,128)(2,1)S(1)}, bf16[16,1,32,4096]{3,2,1,0:T(8,128)(2,1)}, u32[]{:S(2)}) copy-start(bf16[16,1,32,4096]{3,2,1,0:T(8,128)(2,1)} %get-tuple-element.25) | copy-start | bytes 12582916
  421.7 3.3 copy-start.4
  421.7 3.3 copy-start.5
where the time goes:
time: 433 us; the launch traced here: 431 us
  waiting for transfers between devices  191 us (44%)
  other arithmetic  73 us (17%)
  local copies, waits for them, and re-layouts  53.6 us (12%)
  starting transfers between devices  50.1 us (12%)
  blocking collectives  44.6 us (10%)
  matrix products  18.3 us (4%)
    all_to_all x1, waiting for transfers between devices, local(): lax.all_to_all(outgoing, 'cls', split_axis=0, concat_axis=0, tiled=True)  140 us
    all_to_all x1, waiting for transfers between devices, local(): lax.all_to_all(scores, 'cls', split_axis=0, concat_axis=0, tiled=True)  50.2 us
    all_to_all x1, blocking collectives, local(): lax.all_to_all(weight_buffer, 'cls', split_axis=0, concat_axis=0, tiled=T...  44.6 us
    convert_element_type x1, other arithmetic, local(): jnp.where(live_slot, rotation_prior[owner_row], 0).astype(jnp.bfloat16)  40 us
    all_to_all x1, starting transfers between devices, local(): lax.all_to_all(scores, 'cls', split_axis=0, concat_axis=0, tiled=True)  36.5 us
    another operation x5, local copies, waits for them, and re-layouts, local(): scores = jnp.stack(blocks, axis=1)  13.4 us
    dot_general x2, matrix products, score_slots(): jnp.dot(block_spectra, stack.T, preferred_element_type=jnp.float32)  9.77 us
  transfers between devices with their start and end apart: 3, of which 2 were waited for; matrix products, arithmetic and copies ran while one was open for 8% of the time, Pallas kernels for 0%

commit v1 on v0

--- a/solution.py
+++ b/solution.py
@@ -1,3 +1,4 @@
+import functools
 import math
 
 import jax
@@ -10,6 +11,7 @@
 
 
 KAPPA = 2.0
+LOWEST = -1e30
 
 
 def dft_tables(pixels, band_size):
@@ -115,7 +117,7 @@
     return jnp.concatenate([real_running_sum, imaginary_running_sum], axis=-1)
 
 
-def local(
+def routed(
     images, mask_radius, rotation_prior, candidates, references, noise_inverse_power, class_bias
 ):
     row_count = images.shape[0]
@@ -214,6 +216,68 @@
     return (jnp.stack(sum_list, axis=0), jnp.stack(occ_list, axis=0), log_norm)
 
 
+def dense(
+    images, mask_radius, rotation_prior, candidates, references, noise_inverse_power, class_bias
+):
+    row_count, top_count = candidates.shape
+    classes_on_device, rot_count, freq_len = references.shape
+    devices = lax.axis_size("cls")
+    hypotheses = SIDE * SIDE * rot_count
+    me = lax.axis_index("cls")
+    labels = jnp.concatenate([candidates, rotation_prior[:, None]], axis=1)
+    all_labels = lax.all_gather(labels, "cls", axis=0, tiled=True)
+    row_table, col_table = dft_tables(images.shape[1], BAND)
+    spectra = spectra_of(images, mask_radius, row_table, col_table)
+    everyone = lax.all_gather(spectra, "cls", axis=0, tiled=True)
+    cos_t, sin_t = phase_tables(images.shape[1], BAND, SIDE)
+    angle_step = (
+        jnp.arange(rot_count, dtype=jnp.float32)[None, :]
+        - all_labels[:, top_count].astype(jnp.float32)[:, None]
+    )
+    prior_term = KAPPA * jnp.cos(2.0 * math.pi / rot_count * angle_step)
+    prior_term = jnp.tile(prior_term, (1, SIDE * SIDE))
+    scores, names = [], []
+    for c in range(classes_on_device):
+        stack = translated_images(references[c], noise_inverse_power, cos_t, sin_t)
+        penalty = penalty_lookup(references[c], noise_inverse_power)
+        cross = jnp.dot(everyone, stack.T, preferred_element_type=jnp.float32)
+        offset = jnp.tile(class_bias[c] - penalty, SIDE * SIDE)
+        scores.append(cross + offset[None, :] + prior_term)
+        names.append(jnp.any(all_labels[:, :top_count] == me * classes_on_device + c, axis=1))
+    tops = [jnp.where(n, jnp.max(s, axis=1), LOWEST) for s, n in zip(scores, names)]
+    top = functools.reduce(jnp.maximum, tops)
+    mass = sum(
+        jnp.where(n, jnp.sum(jnp.exp(s - jnp.where(n, top, jnp.inf)[:, None]), axis=1), 0.0)
+        for s, n in zip(scores, names)
+    )
+    pairs = lax.all_gather(jnp.stack([top, mass]), "cls", axis=0)
+    peak = jnp.max(pairs[:, 0], axis=0)
+    norm = peak + jnp.log(jnp.sum(pairs[:, 1] * jnp.exp(pairs[:, 0] - peak[None]), axis=0))
+    scale = classes_on_device * rot_count / row_count
+    sums, occ = [], []
+    for s, n in zip(scores, names):
+        limit = jnp.where(n, norm, jnp.inf)
+        weights = jnp.exp(s - limit[:, None]).astype(jnp.bfloat16)
+        occ.append(
+            scale
+            * jnp.sum(
+                weights.astype(jnp.float32).reshape(-1, SIDE * SIDE, rot_count), axis=(0, 1)
+            )
+        )
+        gathered = jnp.einsum("sh,sf->hf", weights, everyone, preferred_element_type=jnp.float32)
+        gathered = gathered.reshape(SIDE * SIDE, rot_count, freq_len)
+        sums.append(shift_back(gathered, cos_t, sin_t) * scale)
+    own = lax.dynamic_slice(norm, (me * row_count,), (row_count,))
+    return (jnp.stack(sums, axis=0), jnp.stack(occ, axis=0), own)
+
+
+def local(*arrays):
+    row_count, top_count = arrays[3].shape
+    classes = arrays[4].shape[0] * lax.axis_size("cls")
+    slots = max(2, 2 * row_count * top_count // classes)
+    return dense(*arrays) if row_count <= 2 * slots else routed(*arrays)
+
+
 def solution(mesh):
     in_specs = (
         P(("parts", "cls"), None, None),

time: 433 us -> 160 us (0.37)
  waiting for transfers between devices: 191 us -> 44.3 us
  other arithmetic: 73 us -> 20.1 us
  starting transfers between devices: 50.1 us -> 0.04 us
  local copies, waits for them, and re-layouts: 53.6 us -> 7.01 us
  between operations: 1.13 us -> 14.4 us
  matrix products: 18.3 us -> 30.6 us
    all_to_all x3 -> x0, waiting for transfers between devices: 191 us -> none  [the longest x1 140 us: local(): lax.all_to_all(outgoing, 'cls', split_axis=0, concat_axis=0, tiled=True)]
    all_to_all x3 -> x0, starting transfers between devices: 50.1 us -> none  [the longest x1 36.5 us: local(): lax.all_to_all(scores, 'cls', split_axis=0, concat_axis=0, tiled=True)]
    all_to_all x1 -> x0, blocking collectives: 44.6 us -> none  [local(): lax.all_to_all(weight_buffer, 'cls', split_axis=0, concat_axis=0, tiled=T...]
    all_gather x0 -> x1, waiting for transfers between devices: none -> 44.3 us  [dense(): everyone = lax.all_gather(spectra, 'cls', axis=0, tiled=True)]
    all_gather x0 -> x2, blocking collectives: none -> 43.4 us  [the longest x1 24.1 us: dense(): all_labels = lax.all_gather(labels, 'cls', axis=0, tiled=True)]
    convert_element_type x3 -> x1, other arithmetic: 41.6 us -> 0.01 us  [dense(): all_labels[:, top_count].astype(jnp.float32)[:, None]]
    gather x7 -> x0, local copies, waits for them, and re-layouts: 22.1 us -> none  [the longest x4 7.79 us: local(): rotation_prior[owner_row]]
    another operation x5 -> x2, local copies, waits for them, and re-layouts: 13.4 us -> 0.01 us  [dense(): offset = jnp.tile(class_bias[c] - penalty, SIDE * SIDE)]
  transfers between devices with their start and end apart: 3 -> 1, of which waited for: 2 -> 1; matrix products, arithmetic and copies ran while one was open for 8% -> 6% of each run, Pallas kernels for 0% -> 0%
where the time goes in v1:
time: 160 us
  waiting for transfers between devices  44.3 us (28%)
  blocking collectives  43.4 us (27%)
  matrix products  30.6 us (19%)
  other arithmetic  20.1 us (13%)
  between operations  14.4 us (9%)
  local copies, waits for them, and re-layouts  7.01 us (4%)
    all_gather x1, waiting for transfers between devices, dense(): everyone = lax.all_gather(spectra, 'cls', axis=0, tiled=True)  44.3 us
    all_gather x1, blocking collectives, dense(): all_labels = lax.all_gather(labels, 'cls', axis=0, tiled=True)  24.1 us
    all_gather x1, blocking collectives, dense(): pairs = lax.all_gather(jnp.stack([top, mass]), 'cls', axis=0)  19.3 us
    dot_general x2, matrix products, dense(): jnp.einsum('sh,sf->hf', weights, everyone, preferred_element_type=jnp.flo...  15.1 us
    dot_general x2, matrix products, dense(): cross = jnp.dot(everyone, stack.T, preferred_element_type=jnp.float32)  14.2 us
    another operation x3, other arithmetic  4.98 us
    dot_general x1, other arithmetic, shift_back(): jnp.einsum('iqz,iz->qz', imaginary_block_part, sine_lookup_matrix, precis...  4.43 us
  transfers between devices with their start and end apart: 1, of which 1 were waited for; matrix products, arithmetic and copies ran while one was open for 6% of the time, Pallas kernels for 0%

profile of v1, /device:TPU:0, one launch (start us, length us, event | category | flops | bytes accessed | tf_op | source)
XLA Modules:
  0.0 159.9 jit_solution(14909562828512514419)
XLA Ops:
  7.3 0.7 mul.673
  8.4 2.1 %compare_select_fusion = bf16[64,128,128]{2,1,0:T(8,128)(2,1)S(1)} fusion(bf16[64,128,128]{2,1,0:T(8,128)(2,1)} %param.7, s32[128,128]{1,0:T(8,128)S(1)} %broadcast_add_fusion.1, s32[64]{0:T(128)S(1)} %mul.673), kind=kLoop, calls=%fused_computation.25 | loop fusion | flops 2097152 | bytes 4260096 | tf_op jit(solution)/shard_map/jit(_where)/select_n | solution.py:44
  10.5 0.8 fusion.12
  11.6 1.1 copy.26
  12.7 0.7 reshape.427
  13.9 1.7 %copy.27 = bf16[64,128,32]{0,2,1:T(8,128)(2,1)S(1)} copy(bf16[64,128,32]{1,2,0:T(8,128)(2,1)S(1)} %fusion.14) | data formatting | bytes 1048576 | tf_op jit(solution)/shard_map/convert_element_type | solution.py:54
  15.7 1.1 copy.28
  17.1 24.1 %all-gather.1 = s32[16,64,9]{1,2,0:T(8,128)S(1)} all-gather(s32[1,64,9]{1,2,0:T(8,128)S(1)} %add_bitcast_fusion.2), channel_id=1, replica_groups=mesh['parts'=2,'cls'=16] {'cls'}, dimensions={0}, use_global_device_ids=true | all-gather | bytes 39168 | tf_op jit(solution)/shard_map/all_gather | solution.py:228
  41.8 0.6 fusion.61
  42.5 0.5 fusion.17
  43.0 1.3 multiply_subtract_fusion
  44.5 0.9 cosine_multiply_fusion
  45.4 0.5 fusion.58
  45.9 4.7 %subtract_convert_fusion.1 = (bf16[9,64,2048]{2,1,0:T(8,128)(2,1)}, bf16[9,64,2048]{2,1,0:T(8,128)(2,1)}, bf16[9,64,2048]{2,1,0:T(8,128)(2,1)}, bf16[9,64,2048]{2,1,0:T(8,128)(2,1)}) fusion(f32[9,2048]{1,0:T(8,128)S(1)} %get-tuple-element.41, f32[64,2048]{1,0:T(8,128)S(1)} %get-tuple-element.35, f32[9,2048]{1,0:T(8,128)S(1)} %get-tuple-element.42, ...), kind=kLoop, calls=%fused_computation.24 | loop fusion | flops 18874368 | bytes 11681792 | tf_op jit(solution)/shard_map/convert.7
  50.6 44.3 %all-gather.5.cloned.1.call-done = bf16[1024,4096]{1,0:T(8,128)(2,1)} async-done(((bf16[64,4096]{1,0:T(8,128)(2,1)}), bf16[1024,4096]{1,0:T(8,128)(2,1)}) %all-gather.5.cloned.1.call-update) | async-done | bytes 8388624 | tf_op jit(solution)/shard_map/all_gather | solution.py:231
  94.8 9.1 %fusion.63 = (f32[1024]{0:T(1024)S(1)}, f32[1024,576]{0,1:T(8,128)S(1)}) fusion(f32[1024,64]{0,1:T(8,128)S(1)} %cosine_multiply_fusion, f32[576]{0:T(1024)S(1)} %add.348, bf16[1024,4096]{1,0:T(8,128)(2,1)} %all-gather.5.cloned.1.call-done, bf16[576,2048]{1,0:T(8,128)(2,1)} %bitcast.126, bf16[576,2048]{1,0:T(8,128)(2,1)} %bitcast.125), kind=kOutput, calls=%fused_computation.145 | convolution fusion | flops 4843043840 | bytes 15735040 | tf_op jit(solution)/shard_map/dot_general | solution.py:243
  104.0 5.1 %fusion.62 = (f32[1024]{0:T(1024)S(1)}, f32[1024,576]{0,1:T(8,128)S(1)}) fusion(f32[1024,64]{0,1:T(8,128)S(1)} %cosine_multiply_fusion, f32[576]{0:T(1024)S(1)} %add.356, bf16[1024,4096]{1,0:T(8,128)(2,1)S(1)} %copy-done.9, bf16[576,2048]{1,0:T(8,128)(2,1)S(1)} %bitcast.123, bf16[576,2048]{1,0:T(8,128)(2,1)S(1)} %bitcast.124), kind=kOutput, calls=%fused_computation.144 | convolution fusion | flops 4843043840 | bytes 15735040 | tf_op jit(solution)/shard_map/dot_general | solution.py:243
  109.9 19.3 %all-gather.2 = f32[16,2,1024]{2,1,0:T(2,128)S(1)} all-gather(f32[1,2,1024]{2,1,0:T(2,128)S(1)} %maximum_bitcast_fusion.2), channel_id=2, replica_groups=mesh['parts'=2,'cls'=16] {'cls'}, dimensions={0}, use_global_device_ids=true | all-gather | bytes 139264 | tf_op jit(solution)/shard_map/all_gather | solution.py:253
  129.4 0.6 dynamic_slice.3
  131.0 0.6 pad_maximum_fusion.1
  131.6 7.6 %fusion.21 = f32[576,4096]{1,0:T(8,128)S(1)} fusion(bf16[1024,4096]{1,0:T(8,128)(2,1)} %all-gather.5.cloned.1.call-done, f32[1024,576]{0,1:T(8,128)S(1)} %get-tuple-element.54, f32[1024]{0:T(1024)S(1)} %get-tuple-element.23), kind=kOutput, calls=%fused_computation.61 | convolution fusion | flops 4833017856 | bytes 20189184 | tf_op jit(solution)/shard_map/sh,sf->hf/dot_general | solution.py:267
  139.2 7.5 %fusion.22 = f32[576,4096]{1,0:T(8,128)S(1)} fusion(bf16[1024,4096]{1,0:T(8,128)(2,1)} %all-gather.5.cloned.1.call-done, f32[1024,576]{0,1:T(8,128)S(1)} %copy-done.1, f32[1024]{0:T(1024)S(1)} %broadcast_select_fusion), kind=kOutput, calls=%fused_computation.62 | convolution fusion | flops 4833017856 | bytes 20189184 | tf_op jit(solution)/shard_map/sh,sf->hf/dot_general | solution.py:267
  146.7 4.4 %multiply_reduce_fusion.2 = (f32[2048,64]{0,1:T(8,128)S(1)}, f32[2048,64]{0,1:T(8,128)S(1)}, f32[2048,64]{0,1:T(8,128)S(1)}, f32[2048,64]{0,1:T(8,128)S(1)}, f32...) fusion(f32[9,64,4096]{2,1,0:T(8,128)S(1)} %bitcast.120, ...), kind=kLoop, calls=%fused_computation.15 | loop fusion | flops 17825792 | bytes 23216128 | tf_op jit(solution)/shard_map/iqz,iz->qz/dot_general | solution.py:111
  151.6 1.5 pad_maximum_fusion
  (72 shorter events, 4.6 us)
Async XLA Ops:
  7.2 87.7 %all-gather.5.cloned.1.call-start = ((), (), s32[]{:S(2)}) async-start(), calls=%async_computation | async-start | bytes 8912896 | tf_op jit(solution)/shard_map/all_gather | solution.py:231
  13.4 3.6 %copy-start.6 = (s32[64,8]{0,1:T(8,128)S(1)}, s32[64,8]{0,1:T(8,128)}, u32[]{:S(2)}) copy-start(s32[64,8]{0,1:T(8,128)} %param.10) | copy-start | bytes 6148
  13.5 3.6 %copy-start.8 = (s32[64]{0:T(128)S(1)}, s32[64]{0:T(128)}, u32[]{:S(2)}) copy-start(s32[64]{0:T(128)} %param.9) | copy-start | bytes 772
  13.9 27.9 %copy-start.7 = (f32[2]{0:T(128)S(1)}, f32[2]{0:T(128)}, u32[]{:S(2)}) copy-start(f32[2]{0:T(128)} %param.13) | copy-start | bytes 28
  13.9 28.4 %copy-start.4 = (bf16[2,64,4096]{2,1,0:T(8,128)(2,1)S(1)}, bf16[2,64,4096]{2,1,0:T(8,128)(2,1)}, u32[]{:S(2)}) copy-start(bf16[2,64,4096]{2,1,0:T(8,128)(2,1)} %param.11) | copy-start | bytes 3145732
  15.6 26.8 %copy-start.5 = (f32[2048]{0:T(1024)S(1)}, f32[2048]{0:T(1024)}, u32[]{:S(2)}) copy-start(f32[2048]{0:T(1024)} %param.12) | copy-start | bytes 24580
  94.8 9.1 %copy-start.2 = (bf16[9,64,2048]{2,1,0:T(8,128)(2,1)S(1)}, bf16[9,64,2048]{2,1,0:T(8,128)(2,1)}, u32[]{:S(2)}) copy-start(bf16[9,64,2048]{2,1,0:T(8,128)(2,1)} %get-tuple-element.37) | copy-start | bytes 7077892
  94.8 9.1 %copy-start.3 = (bf16[9,64,2048]{2,1,0:T(8,128)(2,1)S(1)}, bf16[9,64,2048]{2,1,0:T(8,128)(2,1)}, u32[]{:S(2)}) copy-start(bf16[9,64,2048]{2,1,0:T(8,128)(2,1)} %get-tuple-element.38) | copy-start | bytes 7077892
  94.8 9.1 %copy-start.9 = (bf16[1024,4096]{1,0:T(8,128)(2,1)S(1)}, bf16[1024,4096]{1,0:T(8,128)(2,1)}, u32[]{:S(2)}) copy-start(bf16[1024,4096]{1,0:T(8,128)(2,1)} %all-gather.5.cloned.1.call-done) | copy-start | bytes 25165828
  109.1 20.9 %copy-start = (f32[1024,576]{0,1:T(8,128)}, f32[1024,576]{0,1:T(8,128)S(1)}, u32[]{:S(2)}) copy-start(f32[1024,576]{0,1:T(8,128)S(1)} %get-tuple-element.52) | copy-start | bytes 7077892
  131.6 7.6 %copy-start.1 = (f32[1024,576]{0,1:T(8,128)S(1)}, f32[1024,576]{0,1:T(8,128)}, u32[]{:S(2)}) copy-start(f32[1024,576]{0,1:T(8,128)} %copy-done) | copy-start | bytes 7077892
Sparse Core Ops, SparseCore 0:
  16.9 77.8 all-gather.4

commit v2 on v0

--- a/solution.py
+++ b/solution.py
@@ -1,8 +1,12 @@
+import functools
 import math
 
 import jax
 import jax.numpy as jnp
+import numpy as np
 from jax import lax
+from jax.experimental import pallas as pl
+from jax.experimental.pallas import tpu as pltpu
 from jax.sharding import PartitionSpec as P
 
 BAND = 32
@@ -10,6 +14,7 @@
 
 
 KAPPA = 2.0
+LOWEST = -1e30
 
 
 def dft_tables(pixels, band_size):
@@ -115,7 +120,7 @@
     return jnp.concatenate([real_running_sum, imaginary_running_sum], axis=-1)
 
 
-def local(
+def routed(
     images, mask_radius, rotation_prior, candidates, references, noise_inverse_power, class_bias
 ):
     row_count = images.shape[0]
@@ -214,6 +219,325 @@
     return (jnp.stack(sum_list, axis=0), jnp.stack(occ_list, axis=0), log_norm)
 
 
+def fused_kernel(
+    nd, spec, labs, refs, ninv, cos_t, sin_t, cols, sums, occ, norm_out,
+    everyone, labels, pairs, stack, scores, weights, base,
+    up_sem, down_sem, x_sem, core_sem, recv_sem, lab_send, lab_recv, pair_send, pair_recv,
+):
+    me = lax.axis_index("cls")
+    part = lax.axis_index("parts")
+    nz = nd // 4
+    z, x, c = me // 4, me // 2 % 2, me % 2
+    shifts = cos_t.shape[0]
+    rows = refs.shape[0]
+    half = ninv.shape[1]
+    group = 4 * spec.shape[0]
+
+    def remote(src, dst, send, recv, peer):
+        return pltpu.make_async_remote_copy(
+            src_ref=src, dst_ref=dst, send_sem=send, recv_sem=recv,
+            device_id=(part, peer), device_id_type=pl.DeviceIdType.MESH,
+        )
+
+    barrier = pltpu.get_barrier_semaphore()
+    for k in range(1, nd):
+        pl.semaphore_signal(
+            barrier, inc=1, device_id=(part, (me + k) % nd), device_id_type=pl.DeviceIdType.MESH
+        )
+    pl.semaphore_wait(barrier, nd - 1)
+
+    def block_copy(o, sem, peer):
+        return remote(everyone.at[o], everyone.at[o], sem.at[o], recv_sem.at[o], peer)
+
+    def wait_block(o):
+        block_copy(o, x_sem, (me + 1) % nd).wait_recv()
+
+    def sends(zz, act):
+        o = zz * 4 + x * 2 + c
+
+        @pl.when((zz <= z) & (z + 1 < nz))
+        def _():
+            act(block_copy(o, up_sem, me + 4))
+
+        @pl.when((zz >= z) & (z > 0))
+        def _():
+            act(block_copy(o, down_sem, me - 4))
+
+        act(block_copy(o, x_sem, z * 4 + (1 - x) * 2 + c))
+        act(block_copy(o, core_sem, z * 4 + x * 2 + 1 - c))
+
+    def cross_send(zz, act):
+        o = zz * 4 + (1 - x) * 2 + c
+        act(block_copy(o, core_sem, z * 4 + x * 2 + 1 - c))
+
+    everyone[me] = spec[...]
+    sends(z, lambda d: d.start())
+    labels[me] = labs[...]
+    for k in range(1, nd):
+        peer = (me + k) % nd
+        remote(labs, labels.at[me], lab_send.at[k], lab_recv.at[me], peer).start()
+
+    tile = 512
+    cost = jnp.zeros((rows, 1), jnp.float32)
+    for f in range(0, half, tile):
+        power = ninv[:, f : f + tile]
+        re = refs[:, f : f + tile].astype(jnp.float32)
+        im = refs[:, half + f : half + f + tile].astype(jnp.float32)
+        cost = cost + jnp.sum(power * (re * re + im * im), axis=1, keepdims=True)
+        re = re * power
+        im = im * power
+        for t in range(shifts):
+            ct = cos_t[t : t + 1, f : f + tile]
+            st = sin_t[t : t + 1, f : f + tile]
+            stack[t * rows : (t + 1) * rows, f : f + tile] = (re * ct - im * st).astype(
+                jnp.bfloat16
+            )
+            stack[t * rows : (t + 1) * rows, half + f : half + f + tile] = (
+                re * st + im * ct
+            ).astype(jnp.bfloat16)
+    base[...] = jnp.broadcast_to(cols[:, 0:1] - 0.5 * cost, base.shape)
+    for k in range(1, nd):
+        o = (me + k) % nd
+        remote(labs, labels.at[o], lab_send.at[k], lab_recv.at[o], o).wait_recv()
+
+    def score_group(zz):
+        lanes = pl.ds(pl.multiple_of(zz * group, group), group)
+        first = labels[4 * zz] + labels[4 * zz + 1]
+        second = labels[4 * zz + 2] + labels[4 * zz + 3]
+        lab = jnp.concatenate([first, second], axis=1)
+        top_count = lab.shape[0] - 8
+        mine = cols[:, 3:4]
+        named = lab[0:1, :] == mine
+        for k in range(1, top_count):
+            named = named | (lab[k : k + 1, :] == mine)
+        extra = (
+            base[:, 0:1]
+            + cols[:, 1:2] * lab[top_count : top_count + 1, :]
+            + cols[:, 2:3] * lab[top_count + 1 : top_count + 2, :]
+        )
+        block = everyone[pl.ds(4 * zz, 4)].reshape(group, spec.shape[1])
+        step = 3 * rows
+
+        def chunk(i, top):
+            at = pl.multiple_of(i * step, step)
+            value = lax.dot_general(
+                stack[pl.ds(at, step), :], block, (((1,), (1,)), ((), ())),
+                preferred_element_type=jnp.float32,
+            )
+            for j in range(3):
+                one = jnp.where(named, value[j * rows : (j + 1) * rows] + extra, LOWEST)
+                scores[pl.ds(pl.multiple_of(at + j * rows, rows), rows), lanes] = one
+                top = jnp.maximum(top, one)
+            return top
+
+        top = lax.fori_loop(
+            0, shifts // 3, chunk, jnp.full((rows, group), LOWEST, jnp.float32)
+        )
+        top = jnp.max(top, axis=0, keepdims=True)
+        mass = jnp.zeros((rows, group), jnp.float32)
+        for t in range(shifts):
+            mass = mass + jnp.exp(scores[t * rows : (t + 1) * rows, lanes] - top)
+        pairs[me, 0:1, lanes] = top
+        pairs[me, 1:2, lanes] = jnp.sum(mass, axis=0, keepdims=True)
+
+    def at_distance(s, fn):
+        @pl.when(z - s >= 0)
+        def _():
+            fn(z - s)
+
+        @pl.when((s > 0) & (z + s < nz))
+        def _():
+            fn(z + s)
+
+    def from_column(zz):
+        wait_block(zz * 4 + x * 2 + c)
+        sends(zz, lambda d: d.start())
+
+    def from_side(zz):
+        wait_block(zz * 4 + (1 - x) * 2 + c)
+        cross_send(zz, lambda d: d.start())
+
+    def finish_group(zz):
+        wait_block(zz * 4 + x * 2 + 1 - c)
+        wait_block(zz * 4 + (1 - x) * 2 + 1 - c)
+        score_group(zz)
+
+    def stage(i, carry):
+        @pl.when(i < nz)
+        def _():
+            at_distance(i, from_column)
+
+        at_distance(i - 1, from_side)
+        at_distance(i - 1, finish_group)
+        return carry
+
+    lax.fori_loop(1, nz + 1, stage, 0)
+
+    for k in range(1, nd):
+        peer = (me + k) % nd
+        remote(pairs.at[me], pairs.at[me], pair_send.at[k], pair_recv.at[me], peer).start()
+    for k in range(1, nd):
+        o = (me + k) % nd
+        remote(pairs.at[o], pairs.at[o], pair_send.at[k], pair_recv.at[o], o).wait_recv()
+    peak = pairs[0, 0:1, :]
+    for d in range(1, nd):
+        peak = jnp.maximum(peak, pairs[d, 0:1, :])
+    total = jnp.zeros_like(peak)
+    for d in range(nd):
+        total = total + pairs[d, 1:2, :] * jnp.exp(pairs[d, 0:1, :] - peak)
+    norm = peak + jnp.log(total)
+    norm_out[...] = norm
+    scale = cols[0:1, 4:5]
+
+    def weigh(t, held):
+        at = pl.ds(pl.multiple_of(t * rows, rows), rows)
+        w = jnp.exp(scores[at, :] - norm_out[...]).astype(jnp.bfloat16)
+        weights[at, :] = w
+        return held + jnp.sum(w.astype(jnp.float32), axis=1, keepdims=True)
+
+    held = lax.fori_loop(0, shifts, weigh, jnp.zeros((rows, 1), jnp.float32))
+    occ[...] = jnp.broadcast_to(held * scale, occ.shape)
+
+    wide = 256
+
+    def back(i, carry):
+        at = pl.multiple_of(i * wide, wide)
+        re_at, im_at = pl.ds(at, wide), pl.ds(pl.multiple_of(half + at, wide), wide)
+        re = everyone[:, :, re_at].reshape(-1, wide)
+        im = everyone[:, :, im_at].reshape(-1, wide)
+        g_re = jnp.dot(weights[...], re, preferred_element_type=jnp.float32)
+        g_im = jnp.dot(weights[...], im, preferred_element_type=jnp.float32)
+        out_re = jnp.zeros((rows, wide), jnp.float32)
+        out_im = jnp.zeros((rows, wide), jnp.float32)
+        for t in range(shifts):
+            ct = cos_t[t : t + 1, re_at]
+            st = sin_t[t : t + 1, re_at]
+            a = g_re[t * rows : (t + 1) * rows]
+            b = g_im[t * rows : (t + 1) * rows]
+            out_re = out_re + a * ct + b * st
+            out_im = out_im + b * ct - a * st
+        sums[:, re_at] = out_re * scale
+        sums[:, im_at] = out_im * scale
+        return carry
+
+    lax.fori_loop(0, half // wide, back, 0)
+
+    def settle(zz, carry):
+        sends(zz, lambda d: d.wait_send())
+        cross_send(zz, lambda d: d.wait_send())
+        return carry
+
+    lax.fori_loop(0, nz, settle, 0)
+    for k in range(1, nd):
+        peer = (me + k) % nd
+        remote(labs, labels.at[me], lab_send.at[k], lab_recv.at[me], peer).wait_send()
+        remote(pairs.at[me], pairs.at[me], pair_send.at[k], pair_recv.at[me], peer).wait_send()
+
+
+def phase_constants(pixels, band_size, side_len):
+    fy = np.arange(2 * band_size) - band_size
+    fx = np.arange(band_size)
+    off = np.arange(side_len) - side_len // 2
+    a, b = np.repeat(off, side_len), np.tile(off, side_len)
+    arg = (fy[None, :, None] * a[:, None, None] + fx[None, None, :] * b[:, None, None]) % pixels
+    ang = 2.0 * math.pi / pixels * arg.reshape(side_len * side_len, -1)
+    return np.cos(ang).astype(np.float32), np.sin(ang).astype(np.float32)
+
+
+def dense(
+    images, mask_radius, rotation_prior, candidates, references, noise_inverse_power, class_bias
+):
+    row_count, top_count = candidates.shape
+    classes_on_device, rot_count, freq_len = references.shape
+    devices = lax.axis_size("cls")
+    me = lax.axis_index("cls")
+    particles = devices * row_count
+    rows = classes_on_device * rot_count
+    shifts = SIDE * SIDE
+    row_table, col_table = dft_tables(images.shape[1], BAND)
+    spectra = spectra_of(images, mask_radius, row_table, col_table)
+    cos_t, sin_t = phase_constants(images.shape[1], BAND, SIDE)
+    turn = 2.0 * math.pi / rot_count
+    angle = turn * rotation_prior.astype(jnp.float32)
+    labs = jnp.concatenate(
+        [
+            candidates.T.astype(jnp.float32),
+            KAPPA * jnp.cos(angle)[None],
+            KAPPA * jnp.sin(angle)[None],
+            jnp.zeros((6, row_count), jnp.float32),
+        ],
+        axis=0,
+    )
+    blank = jnp.zeros_like(labs)
+    labs = jnp.where(
+        me % 2 == 0,
+        jnp.concatenate([labs, blank], axis=1),
+        jnp.concatenate([blank, labs], axis=1),
+    )
+    r = np.arange(rows) % rot_count
+    own = (me * classes_on_device + jnp.arange(rows) // rot_count).astype(jnp.float32)
+    scale = classes_on_device * rot_count / row_count
+    cols = jnp.stack(
+        [
+            jnp.repeat(class_bias, rot_count),
+            jnp.asarray(np.cos(turn * r), jnp.float32),
+            jnp.asarray(np.sin(turn * r), jnp.float32),
+            own,
+            jnp.full((rows,), scale, jnp.float32),
+        ],
+        axis=1,
+    )
+    cols = jnp.pad(cols, ((0, 0), (0, 123)))
+    vmem = pl.BlockSpec(memory_space=pltpu.VMEM)
+    dma = pltpu.SemaphoreType.DMA((devices,))
+    sums, occ, norm = pl.pallas_call(
+        functools.partial(fused_kernel, devices),
+        out_shape=(
+            jax.ShapeDtypeStruct((rows, freq_len), jnp.float32),
+            jax.ShapeDtypeStruct((rows, 128), jnp.float32),
+            jax.ShapeDtypeStruct((1, particles), jnp.float32),
+        ),
+        in_specs=[vmem] * 7,
+        out_specs=(vmem, vmem, vmem),
+        scratch_shapes=[
+            pltpu.VMEM((devices, row_count, freq_len), jnp.bfloat16),
+            pltpu.VMEM((devices,) + labs.shape, jnp.float32),
+            pltpu.VMEM((devices, 2, particles), jnp.float32),
+            pltpu.VMEM((shifts * rows, freq_len), jnp.bfloat16),
+            pltpu.VMEM((shifts * rows, particles), jnp.float32),
+            pltpu.VMEM((shifts * rows, particles), jnp.bfloat16),
+            pltpu.VMEM((rows, 128), jnp.float32),
+        ]
+        + [dma] * 9,
+        compiler_params=pltpu.CompilerParams(
+            collective_id=0, has_side_effects=True, vmem_limit_bytes=52 * 1024 * 1024
+        ),
+    )(
+        spectra,
+        labs,
+        references.reshape(rows, freq_len),
+        noise_inverse_power[None],
+        jnp.asarray(cos_t),
+        jnp.asarray(sin_t),
+        cols,
+    )
+    own_norm = lax.dynamic_slice(norm[0], (me * row_count,), (row_count,))
+    return (
+        sums.reshape(classes_on_device, rot_count, freq_len),
+        occ[:, 0].reshape(classes_on_device, rot_count),
+        own_norm,
+    )
+
+
+def local(*arrays):
+    row_count, top_count = arrays[3].shape
+    devices = lax.axis_size("cls")
+    classes = arrays[4].shape[0] * devices
+    slots = max(2, 2 * row_count * top_count // classes)
+    fits = row_count == 64 and devices % 4 == 0 and row_count <= 2 * slots
+    return dense(*arrays) if fits else routed(*arrays)
+
+
 def solution(mesh):
     in_specs = (
         P(("parts", "cls"), None, None),

time: 433 us -> 102 us (0.24)
  waiting for transfers between devices: 191 us -> 0 us
  Pallas kernels: 0 us -> 84.7 us
  other arithmetic: 73 us -> 4.82 us
  starting transfers between devices: 50.1 us -> 0 us
  blocking collectives: 44.6 us -> 0 us
  local copies, waits for them, and re-layouts: 53.6 us -> 10.5 us
  matrix products: 18.3 us -> 1.29 us
    all_to_all x3 -> x0, waiting for transfers between devices: 191 us -> none  [the longest x1 140 us: local(): lax.all_to_all(outgoing, 'cls', split_axis=0, concat_axis=0, tiled=True)]
    pallas_call x0 -> x1, Pallas kernels: none -> 84.7 us  [dense(): pl.pallas_call(functools.partial(fused_kernel, devices), out_shape=(jax.S...]
    all_to_all x3 -> x0, starting transfers between devices: 50.1 us -> none  [the longest x1 36.5 us: local(): lax.all_to_all(scores, 'cls', split_axis=0, concat_axis=0, tiled=True)]
    all_to_all x1 -> x0, blocking collectives: 44.6 us -> none  [local(): lax.all_to_all(weight_buffer, 'cls', split_axis=0, concat_axis=0, tiled=T...]
    convert_element_type x3 -> x2, other arithmetic: 41.6 us -> 0.7 us  [the longest x1 0.69 us: dense(): candidates.T.astype(jnp.float32)]
    gather x7 -> x0, local copies, waits for them, and re-layouts: 22.1 us -> none  [the longest x4 7.79 us: local(): rotation_prior[owner_row]]
    dot_general x4 -> x0, matrix products: 17 us -> none  [the longest x2 9.77 us: score_slots(): jnp.dot(block_spectra, stack.T, preferred_element_type=jnp.float32)]
    another operation x6 -> x5, local copies, waits for them, and re-layouts: 13.4 us -> 1.55 us  [the longest x4 0.89 us: dense(): jnp.stack([jnp.repeat(class_bias, rot_count), jnp.asarray(np.cos(turn * r...]
  transfers between devices with their start and end apart: 3 -> 0, of which waited for: 2 -> 0; matrix products, arithmetic and copies ran while one was open for 8% -> 0% of each run, Pallas kernels for 0% -> 0%
where the time goes in v2:
time: 102 us
  Pallas kernels  84.7 us (83%)
  local copies, waits for them, and re-layouts  10.5 us (10%)
  other arithmetic  4.82 us (5%)
  matrix products  1.29 us (1%)
    pallas_call x1, Pallas kernels, dense(): pl.pallas_call(functools.partial(fused_kernel, devices), out_shape=(jax.S...  84.7 us
    unnamed x10, local copies, waits for them, and re-layouts  3.41 us
    select_n x1, other arithmetic, spectra_of(): masked = jnp.where(inside, images, jnp.zeros((), jnp.bfloat16))  2.15 us

profile of v2, /device:TPU:0, one launch (start us, length us, event | category | flops | bytes accessed | tf_op | source)
XLA Modules:
  0.0 102.1 jit_solution(4024663672182108961)
XLA Ops:
  0.7 0.7 mul.112
  1.5 0.7 broadcast_in_dim.12
  2.2 0.1 stack_reshape.3
  2.3 0.7 multiply_bitcast_fusion.1
  3.0 0.7 stack.12
  3.7 0.7 convert_bitcast_fusion
  4.5 0.1 pad_select_fusion.labs
  4.5 0.1 negate_convert_fusion.1
  4.6 0.2 fusion.22
  4.9 0.1 copy.27
  5.0 0.1 broadcast_add_fusion
  5.1 2.1 %compare_select_fusion = bf16[64,128,128]{2,1,0:T(8,128)(2,1)S(1)} fusion(bf16[64,128,128]{2,1,0:T(8,128)(2,1)} %param.11, s32[128,128]{1,0:T(8,128)S(1)} %broadcast_add_fusion, s32[64]{0:T(128)S(1)} %mul.112), kind=kLoop, calls=%fused_computation.1 | loop fusion | flops 2097152 | bytes 4260096 | tf_op jit(solution)/shard_map/jit(_where)/select_n | solution.py:47
  7.2 0.9 fusion
  8.1 0.3 copy.29
  8.4 1.1 %copy.25 = bf16[64,2,128,32]{2,1,3,0:T(2,128)(2,1)S(1)} copy(bf16[64,2,128,32]{2,0,3,1:T(8,128)(2,1)S(1)} %bitcast.34) | data formatting | bytes 2097152 | tf_op jit(solution)/shard_map/transpose | solution.py:52
  9.4 0.9 reshape.112
  10.4 0.4 fusion.2
  10.8 1.7 %copy.26 = bf16[64,128,32]{0,2,1:T(8,128)(2,1)S(1)} copy(bf16[64,128,32]{1,2,0:T(8,128)(2,1)S(1)} %fusion.2) | data formatting | bytes 1048576 | tf_op jit(solution)/shard_map/convert_element_type | solution.py:57
  12.5 0.3 copy.28.spec
  12.9 84.7 %shard_map.130 = (f32[128,4096]{1,0:T(8,128)}, f32[128,128]{1,0:T(8,128)S(1)}, f32[1,1024]{1,0:T(1,128)S(1)}) custom-call(bf16[64,4096]{1,0:T(8,128)(2,1)S(1)} %copy.28.spec, f32[16,128]{1,0:T(8,128)S(1)} %pad_select_fusion.labs, bf16[128,4096]{1,0:T(8,128)(2,1)S(1)} %bitcast.30, f32[1,2048]{1,0:T(1,128)S(1)} %bitcast.31, f32[9,2048]{1,0:T(8,128)S(1)} %copy-done.2, ...), custom_call_target="tpu_custom_call" | custom-call | tf_op jit(solution)/shard_map/pallas_call | solution.py:493
  97.6 0.6 dynamic-slice_bitcast_fusion
  98.2 0.1 slice_reduce_fusion
  98.3 0.7 reshape_squeeze.3
  99.0 3.1 %copy.31 = f32[2,64,4096]{2,1,0:T(8,128)} copy(f32[2,64,4096]{2,1,0:T(8,128)} %bitcast.35) | data formatting | bytes 4194304
  (16 shorter events, 0.2 us)
Async XLA Ops:
  10.3 2.5 %copy-start = (bf16[2,64,4096]{2,1,0:T(8,128)(2,1)S(1)}, bf16[2,64,4096]{2,1,0:T(8,128)(2,1)}, u32[]{:S(2)}) copy-start(bf16[2,64,4096]{2,1,0:T(8,128)(2,1)} %param.15) | copy-start | bytes 3145732
  10.4 2.5 %copy-start.1 = (f32[9,2048]{1,0:T(8,128)S(1)}, f32[9,2048]{1,0:T(8,128)}, u32[]{:S(2)}) copy-start(f32[9,2048]{1,0:T(8,128)} %constant.94.clone.sin_t) | copy-start | bytes 221188
  10.4 2.5 %copy-start.2 = (f32[9,2048]{1,0:T(8,128)S(1)}, f32[9,2048]{1,0:T(8,128)}, u32[]{:S(2)}) copy-start(f32[9,2048]{1,0:T(8,128)} %constant.93.clone.cos_t) | copy-start | bytes 221188
  10.4 2.5 %copy-start.3 = (f32[2048]{0:T(1024)S(1)}, f32[2048]{0:T(1024)}, u32[]{:S(2)}) copy-start(f32[2048]{0:T(1024)} %param.16) | copy-start | bytes 24580

commit v3 on v2

--- a/solution.py
+++ b/solution.py
@@ -15,6 +15,7 @@
 
 KAPPA = 2.0
 LOWEST = -1e30
+LATE = 20
 
 
 def dft_tables(pixels, band_size):
@@ -220,9 +221,9 @@
 
 
 def fused_kernel(
-    nd, spec, labs, refs, ninv, cos_t, sin_t, cols, sums, occ, norm_out,
-    everyone, labels, pairs, stack, scores, weights, base,
-    up_sem, down_sem, x_sem, core_sem, recv_sem, lab_send, lab_recv, pair_send, pair_recv,
+    nd, spec, names, refs, ninv, cos_t, sin_t, cols, bias, sums, occ, norm_out,
+    everyone, labels, pairs, stack, scores, weights, base, labs,
+    up_sem, down_sem, x_sem, core_sem, recv_sem, late_sem, lab_send, lab_recv, pair_send, pair_recv,
 ):
     me = lax.axis_index("cls")
     part = lax.axis_index("parts")
@@ -232,6 +233,7 @@
     rows = refs.shape[0]
     half = ninv.shape[1]
     group = 4 * spec.shape[0]
+    keep = spec.shape[1] - spec.shape[1] * LATE // 128 // 128 * 128
 
     def remote(src, dst, send, recv, peer):
         return pltpu.make_async_remote_copy(
@@ -252,6 +254,25 @@
     def wait_block(o):
         block_copy(o, x_sem, (me + 1) % nd).wait_recv()
 
+    def late_copy(o, sem, peer):
+        piece = everyone.at[o, :, keep:]
+        return remote(piece, piece, sem.at[o], late_sem.at[o], peer)
+
+    def late_sends(zz, act):
+        o = zz * 4 + (1 - x) * 2 + c
+
+        @pl.when((zz <= z) & (z + 1 < nz))
+        def _():
+            act(late_copy(o, up_sem, me + 4))
+
+        @pl.when((zz >= z) & (z > 0))
+        def _():
+            act(late_copy(o, down_sem, me - 4))
+
+    def side_copy(o, peer):
+        piece = everyone.at[o, :, :keep]
+        return remote(piece, piece, x_sem.at[o], recv_sem.at[o], peer)
+
     def sends(zz, act):
         o = zz * 4 + x * 2 + c
 
@@ -263,7 +284,14 @@
         def _():
             act(block_copy(o, down_sem, me - 4))
 
-        act(block_copy(o, x_sem, z * 4 + (1 - x) * 2 + c))
+        @pl.when(zz == z)
+        def _():
+            act(block_copy(o, x_sem, z * 4 + (1 - x) * 2 + c))
+
+        @pl.when(zz != z)
+        def _():
+            act(side_copy(o, z * 4 + (1 - x) * 2 + c))
+
         act(block_copy(o, core_sem, z * 4 + x * 2 + 1 - c))
 
     def cross_send(zz, act):
@@ -272,6 +300,13 @@
 
     everyone[me] = spec[...]
     sends(z, lambda d: d.start())
+    count = names.shape[0]
+    place = lax.broadcasted_iota(jnp.int32, (count, 2 * count), 1) - count * c
+    place = place == lax.broadcasted_iota(jnp.int32, (count, 2 * count), 0)
+    labs[...] = lax.dot_general(
+        names[...], place.astype(jnp.float32).astype(jnp.bfloat16), (((0,), (0,)), ((), ())),
+        preferred_element_type=jnp.float32,
+    )
     labels[me] = labs[...]
     for k in range(1, nd):
         peer = (me + k) % nd
@@ -295,7 +330,11 @@
             stack[t * rows : (t + 1) * rows, half + f : half + f + tile] = (
                 re * st + im * ct
             ).astype(jnp.bfloat16)
-    base[...] = jnp.broadcast_to(cols[:, 0:1] - 0.5 * cost, base.shape)
+    own = cols[:, 2:3]
+    offset = -0.5 * cost
+    for k in range(bias.shape[0]):
+        offset = offset + jnp.where(own == k, bias[k], 0.0)
+    base[...] = jnp.broadcast_to(offset, base.shape)
     for k in range(1, nd):
         o = (me + k) % nd
         remote(labs, labels.at[o], lab_send.at[k], lab_recv.at[o], o).wait_recv()
@@ -306,14 +345,15 @@
         second = labels[4 * zz + 2] + labels[4 * zz + 3]
         lab = jnp.concatenate([first, second], axis=1)
         top_count = lab.shape[0] - 8
-        mine = cols[:, 3:4]
+        mine = cols[:, 2:3] + (me * bias.shape[0]).astype(jnp.float32)
         named = lab[0:1, :] == mine
         for k in range(1, top_count):
             named = named | (lab[k : k + 1, :] == mine)
+        angle = 2.0 * math.pi / (rows // bias.shape[0]) * lab[top_count : top_count + 1, :]
         extra = (
             base[:, 0:1]
-            + cols[:, 1:2] * lab[top_count : top_count + 1, :]
-            + cols[:, 2:3] * lab[top_count + 1 : top_count + 2, :]
+            + cols[:, 0:1] * (KAPPA * jnp.cos(angle))
+            + cols[:, 1:2] * (KAPPA * jnp.sin(angle))
         )
         block = everyone[pl.ds(4 * zz, 4)].reshape(group, spec.shape[1])
         step = 3 * rows
@@ -353,8 +393,26 @@
         wait_block(zz * 4 + x * 2 + c)
         sends(zz, lambda d: d.start())
 
+    def from_late(zz):
+        o = zz * 4 + (1 - x) * 2 + c
+
+        @pl.when(zz == z)
+        def _():
+            wait_block(o)
+
+        @pl.when(zz != z)
+        def _():
+            late_copy(o, up_sem, (me + 1) % nd).wait_recv()
+
+        late_sends(zz, lambda d: d.start())
+
     def from_side(zz):
-        wait_block(zz * 4 + (1 - x) * 2 + c)
+        o = zz * 4 + (1 - x) * 2 + c
+
+        @pl.when(zz != z)
+        def _():
+            side_copy(o, (me + 1) % nd).wait_recv()
+
         cross_send(zz, lambda d: d.start())
 
     def finish_group(zz):
@@ -367,6 +425,7 @@
         def _():
             at_distance(i, from_column)
 
+        at_distance(i - 1, from_late)
         at_distance(i - 1, from_side)
         at_distance(i - 1, finish_group)
         return carry
@@ -387,7 +446,7 @@
         total = total + pairs[d, 1:2, :] * jnp.exp(pairs[d, 0:1, :] - peak)
     norm = peak + jnp.log(total)
     norm_out[...] = norm
-    scale = cols[0:1, 4:5]
+    scale = bias.shape[0] * (rows // bias.shape[0]) / count
 
     def weigh(t, held):
         at = pl.ds(pl.multiple_of(t * rows, rows), rows)
@@ -416,14 +475,15 @@
             b = g_im[t * rows : (t + 1) * rows]
             out_re = out_re + a * ct + b * st
             out_im = out_im + b * ct - a * st
-        sums[:, re_at] = out_re * scale
-        sums[:, im_at] = out_im * scale
+        sums[:, re_at] = out_re
+        sums[:, im_at] = out_im
         return carry
 
     lax.fori_loop(0, half // wide, back, 0)
 
     def settle(zz, carry):
         sends(zz, lambda d: d.wait_send())
+        late_sends(zz, lambda d: d.wait_send())
         cross_send(zz, lambda d: d.wait_send())
         return carry
 
@@ -457,37 +517,13 @@
     row_table, col_table = dft_tables(images.shape[1], BAND)
     spectra = spectra_of(images, mask_radius, row_table, col_table)
     cos_t, sin_t = phase_constants(images.shape[1], BAND, SIDE)
-    turn = 2.0 * math.pi / rot_count
-    angle = turn * rotation_prior.astype(jnp.float32)
-    labs = jnp.concatenate(
-        [
-            candidates.T.astype(jnp.float32),
-            KAPPA * jnp.cos(angle)[None],
-            KAPPA * jnp.sin(angle)[None],
-            jnp.zeros((6, row_count), jnp.float32),
-        ],
-        axis=0,
-    )
-    blank = jnp.zeros_like(labs)
-    labs = jnp.where(
-        me % 2 == 0,
-        jnp.concatenate([labs, blank], axis=1),
-        jnp.concatenate([blank, labs], axis=1),
-    )
-    r = np.arange(rows) % rot_count
-    own = (me * classes_on_device + jnp.arange(rows) // rot_count).astype(jnp.float32)
+    names = jnp.concatenate([candidates, rotation_prior[:, None]], axis=1)
+    names = jnp.pad(names, ((0, 0), (0, 7))).astype(jnp.bfloat16)
+    r = np.arange(rows)
+    turn = 2.0 * math.pi / rot_count * (r % rot_count)
+    cols = np.zeros((rows, 128), np.float32)
+    cols[:, 0], cols[:, 1], cols[:, 2] = np.cos(turn), np.sin(turn), r // rot_count
     scale = classes_on_device * rot_count / row_count
-    cols = jnp.stack(
-        [
-            jnp.repeat(class_bias, rot_count),
-            jnp.asarray(np.cos(turn * r), jnp.float32),
-            jnp.asarray(np.sin(turn * r), jnp.float32),
-            own,
-            jnp.full((rows,), scale, jnp.float32),
-        ],
-        axis=1,
-    )
-    cols = jnp.pad(cols, ((0, 0), (0, 123)))
     vmem = pl.BlockSpec(memory_space=pltpu.VMEM)
     dma = pltpu.SemaphoreType.DMA((devices,))
     sums, occ, norm = pl.pallas_call(
@@ -497,33 +533,35 @@
             jax.ShapeDtypeStruct((rows, 128), jnp.float32),
             jax.ShapeDtypeStruct((1, particles), jnp.float32),
         ),
-        in_specs=[vmem] * 7,
+        in_specs=[vmem] * 7 + [pl.BlockSpec(memory_space=pltpu.SMEM)],
         out_specs=(vmem, vmem, vmem),
         scratch_shapes=[
             pltpu.VMEM((devices, row_count, freq_len), jnp.bfloat16),
-            pltpu.VMEM((devices,) + labs.shape, jnp.float32),
+            pltpu.VMEM((devices, top_count + 8, 2 * row_count), jnp.float32),
             pltpu.VMEM((devices, 2, particles), jnp.float32),
             pltpu.VMEM((shifts * rows, freq_len), jnp.bfloat16),
             pltpu.VMEM((shifts * rows, particles), jnp.float32),
             pltpu.VMEM((shifts * rows, particles), jnp.bfloat16),
             pltpu.VMEM((rows, 128), jnp.float32),
+            pltpu.VMEM((top_count + 8, 2 * row_count), jnp.float32),
         ]
-        + [dma] * 9,
+        + [dma] * 10,
         compiler_params=pltpu.CompilerParams(
             collective_id=0, has_side_effects=True, vmem_limit_bytes=52 * 1024 * 1024
         ),
     )(
         spectra,
-        labs,
+        names,
         references.reshape(rows, freq_len),
         noise_inverse_power[None],
         jnp.asarray(cos_t),
         jnp.asarray(sin_t),
-        cols,
+        jnp.asarray(cols),
+        class_bias,
     )
     own_norm = lax.dynamic_slice(norm[0], (me * row_count,), (row_count,))
     return (
-        sums.reshape(classes_on_device, rot_count, freq_len),
+        sums.reshape(classes_on_device, rot_count, freq_len) * scale,
         occ[:, 0].reshape(classes_on_device, rot_count),
         own_norm,
     )

time: 102 us -> 99.7 us (0.977)
  local copies, waits for them, and re-layouts: 10.5 us -> 5.79 us
  other arithmetic: 4.82 us -> 7.74 us
    unnamed x10 -> x13, local copies, waits for them, and re-layouts: 3.41 us -> 0.31 us
    mul x1, other arithmetic: 0.7 us -> 3.1 us  [dense(): sums.reshape(classes_on_device, rot_count, freq_len) * scale]
where the time goes in v3:
time: 99.7 us; the launch traced here: 99.5 us
  Pallas kernels  83.8 us (84%)
  other arithmetic  7.74 us (8%)
  local copies, waits for them, and re-layouts  5.79 us (6%)
  matrix products  1.28 us (1%)
    pallas_call x1, Pallas kernels, dense(): pl.pallas_call(functools.partial(fused_kernel, devices), out_shape=(jax.S...  83.8 us
    mul x1, other arithmetic, dense(): sums.reshape(classes_on_device, rot_count, freq_len) * scale  3.1 us
    select_n x1, other arithmetic, spectra_of(): masked = jnp.where(inside, images, jnp.zeros((), jnp.bfloat16))  2.15 us
    convert_element_type x2, local copies, waits for them, and re-layouts, spectra_of(): whole.reshape(row_count, 4 * band_size * band_size).astype(jnp.bfloat16)  2.04 us

profile of v3, /device:TPU:0, one launch (start us, length us, event | category | flops | bytes accessed | tf_op | source)
XLA Modules:
  0.0 99.5 jit_solution(1864231906252331330)
XLA Ops:
  0.6 0.7 mul.100
  1.4 0.7 convert_bitcast_fusion
  2.0 0.7 convert.34
  2.7 0.1 copy.28
  2.9 0.1 negate_convert_fusion.1
  3.0 0.2 fusion.22
  3.2 0.1 broadcast_add_fusion
  3.3 2.1 %compare_select_fusion = bf16[64,128,128]{2,1,0:T(8,128)(2,1)S(1)} fusion(bf16[64,128,128]{2,1,0:T(8,128)(2,1)} %param.10, s32[128,128]{1,0:T(8,128)S(1)} %broadcast_add_fusion, s32[64]{0:T(128)S(1)} %mul.100), kind=kLoop, calls=%fused_computation.1 | loop fusion | flops 2097152 | bytes 4260096 | tf_op jit(solution)/shard_map/jit(_where)/select_n | solution.py:48
  5.4 0.8 fusion
  6.3 0.3 copy.30
  6.5 1.1 %copy.26 = bf16[64,2,128,32]{2,1,3,0:T(2,128)(2,1)S(1)} copy(bf16[64,2,128,32]{2,0,3,1:T(8,128)(2,1)S(1)} %bitcast.30) | data formatting | bytes 2097152 | tf_op jit(solution)/shard_map/transpose | solution.py:53
  7.6 0.9 reshape.70
  8.5 0.0 copy-start.1
  8.6 0.0 copy-start.2
  8.6 0.0 copy-start.3
  8.6 0.0 copy-start.5
  8.6 0.4 fusion.2
  9.0 1.7 %copy.27 = bf16[64,128,32]{0,2,1:T(8,128)(2,1)S(1)} copy(bf16[64,128,32]{1,2,0:T(8,128)(2,1)S(1)} %fusion.2) | data formatting | bytes 1048576 | tf_op jit(solution)/shard_map/convert_element_type | solution.py:58
  10.7 0.3 copy.29.spec
  11.2 83.8 %shard_map.121 = (f32[128,4096]{1,0:T(8,128)}, f32[128,128]{1,0:T(8,128)S(1)}, f32[1,1024]{1,0:T(1,128)S(1)}) custom-call(bf16[64,4096]{1,0:T(8,128)(2,1)S(1)} %copy.29.spec, bf16[64,16]{1,0:T(8,128)(2,1)S(1)} %pad.5.names, bf16[128,4096]{1,0:T(8,128)(2,1)S(1)} %bitcast.26, f32[1,2048]{1,0:T(1,128)S(1)} %bitcast.27, f32[9,2048]{1,0:T(8,128)S(1)} %copy-done.2, ...), custom_call_target="tpu_custom_call" | custom-call | tf_op jit(solution)/shard_map/pallas_call | solution.py:529
  95.0 0.6 dynamic-slice_bitcast_fusion
  95.6 3.1 %broadcast_multiply_fusion = f32[128,4096]{1,0:T(8,128)} fusion(f32[128,4096]{1,0:T(8,128)} %get-tuple-element.6), kind=kLoop, calls=%fused_computation.6 | loop fusion | flops 524288 | bytes 4194304 | tf_op jit(solution)/shard_map/mul | solution.py:564
  98.7 0.1 slice_reduce_fusion
  98.8 0.7 reshape_squeeze.3
  (12 shorter events, 0.0 us)
Async XLA Ops:
  8.5 2.6 %copy-start = (bf16[2,64,4096]{2,1,0:T(8,128)(2,1)S(1)}, bf16[2,64,4096]{2,1,0:T(8,128)(2,1)}, u32[]{:S(2)}) copy-start(bf16[2,64,4096]{2,1,0:T(8,128)(2,1)} %param.14) | copy-start | bytes 3145732
  8.5 2.6 %copy-start.1 = (f32[9,2048]{1,0:T(8,128)S(1)}, f32[9,2048]{1,0:T(8,128)}, u32[]{:S(2)}) copy-start(f32[9,2048]{1,0:T(8,128)} %constant.57.clone.sin_t) | copy-start | bytes 221188
  8.6 2.6 %copy-start.2 = (f32[9,2048]{1,0:T(8,128)S(1)}, f32[9,2048]{1,0:T(8,128)}, u32[]{:S(2)}) copy-start(f32[9,2048]{1,0:T(8,128)} %constant.56.clone.cos_t) | copy-start | bytes 221188
  8.6 2.6 %copy-start.3 = (f32[128,128]{1,0:T(8,128)S(1)}, f32[128,128]{1,0:T(8,128)}, u32[]{:S(2)}) copy-start(f32[128,128]{1,0:T(8,128)} %constant.58.clone.cols) | copy-start | bytes 196612
  8.6 2.5 %copy-start.4 = (f32[2048]{0:T(1024)S(1)}, f32[2048]{0:T(1024)}, u32[]{:S(2)}) copy-start(f32[2048]{0:T(1024)} %param.15) | copy-start | bytes 24580
  8.6 2.5 %copy-start.5 = (f32[2]{0:T(128)S(1)}, f32[2]{0:T(128)}, u32[]{:S(2)}) copy-start(f32[2]{0:T(128)} %bias.1) | copy-start | bytes 28

commit v4 on v3

--- a/solution.py
+++ b/solution.py
@@ -15,7 +15,7 @@
 
 KAPPA = 2.0
 LOWEST = -1e30
-LATE = 20
+LATE = 8
 
 
 def dft_tables(pixels, band_size):
@@ -479,7 +479,7 @@
         sums[:, im_at] = out_im
         return carry
 
-    lax.fori_loop(0, half // wide, back, 0)
+    lax.fori_loop(0, half // wide, back, 0, unroll=2)
 
     def settle(zz, carry):
         sends(zz, lambda d: d.wait_send())

time: 99.7 us -> 99.8 us (level)
  no operation moved by 1% of the time
where the time goes in v4:
time: 99.8 us; the launch traced here: 99.6 us
  Pallas kernels  84 us (84%)
  other arithmetic  7.74 us (8%)
  local copies, waits for them, and re-layouts  5.79 us (6%)
  matrix products  1.28 us (1%)
    pallas_call x1, Pallas kernels, dense(): pl.pallas_call(functools.partial(fused_kernel, devices), out_shape=(jax.S...  84 us
    mul x1, other arithmetic, dense(): sums.reshape(classes_on_device, rot_count, freq_len) * scale  3.1 us
    select_n x1, other arithmetic, spectra_of(): masked = jnp.where(inside, images, jnp.zeros((), jnp.bfloat16))  2.15 us
    convert_element_type x2, local copies, waits for them, and re-layouts, spectra_of(): whole.reshape(row_count, 4 * band_size * band_size).astype(jnp.bfloat16)  2.04 us

profile of v4, /device:TPU:0, one launch (start us, length us, event | category | flops | bytes accessed | tf_op | source)
XLA Modules:
  0.0 99.6 jit_solution(14819409270904202968)
XLA Ops:
  0.6 0.7 mul.100
  1.4 0.7 convert_bitcast_fusion
  2.0 0.7 convert.34
  2.7 0.1 copy.28
  2.9 0.1 negate_convert_fusion.1
  3.0 0.2 fusion.22
  3.2 0.1 broadcast_add_fusion
  3.3 2.1 %compare_select_fusion = bf16[64,128,128]{2,1,0:T(8,128)(2,1)S(1)} fusion(bf16[64,128,128]{2,1,0:T(8,128)(2,1)} %param.10, s32[128,128]{1,0:T(8,128)S(1)} %broadcast_add_fusion, s32[64]{0:T(128)S(1)} %mul.100), kind=kLoop, calls=%fused_computation.1 | loop fusion | flops 2097152 | bytes 4260096 | tf_op jit(solution)/shard_map/jit(_where)/select_n | solution.py:48
  5.4 0.8 fusion
  6.3 0.3 copy.30
  6.5 1.1 %copy.26 = bf16[64,2,128,32]{2,1,3,0:T(2,128)(2,1)S(1)} copy(bf16[64,2,128,32]{2,0,3,1:T(8,128)(2,1)S(1)} %bitcast.30) | data formatting | bytes 2097152 | tf_op jit(solution)/shard_map/transpose | solution.py:53
  7.6 0.9 reshape.70
  8.5 0.0 copy-start
  8.5 0.0 copy-start.1
  8.6 0.0 copy-start.2
  8.6 0.0 copy-start.3
  8.6 0.4 fusion.2
  9.0 1.7 %copy.27 = bf16[64,128,32]{0,2,1:T(8,128)(2,1)S(1)} copy(bf16[64,128,32]{1,2,0:T(8,128)(2,1)S(1)} %fusion.2) | data formatting | bytes 1048576 | tf_op jit(solution)/shard_map/convert_element_type | solution.py:58
  10.7 0.3 copy.29.spec
  11.2 84.0 %shard_map.121 = (f32[128,4096]{1,0:T(8,128)}, f32[128,128]{1,0:T(8,128)S(1)}, f32[1,1024]{1,0:T(1,128)S(1)}) custom-call(bf16[64,4096]{1,0:T(8,128)(2,1)S(1)} %copy.29.spec, bf16[64,16]{1,0:T(8,128)(2,1)S(1)} %pad.5.names, bf16[128,4096]{1,0:T(8,128)(2,1)S(1)} %bitcast.26, f32[1,2048]{1,0:T(1,128)S(1)} %bitcast.27, f32[9,2048]{1,0:T(8,128)S(1)} %copy-done.2, ...), custom_call_target="tpu_custom_call" | custom-call | tf_op jit(solution)/shard_map/pallas_call | solution.py:529
  95.1 0.6 dynamic-slice_bitcast_fusion
  95.7 3.1 %broadcast_multiply_fusion = f32[128,4096]{1,0:T(8,128)} fusion(f32[128,4096]{1,0:T(8,128)} %get-tuple-element.6), kind=kLoop, calls=%fused_computation.6 | loop fusion | flops 524288 | bytes 4194304 | tf_op jit(solution)/shard_map/mul | solution.py:564
  98.8 0.1 slice_reduce_fusion
  98.9 0.7 reshape_squeeze.3
  (12 shorter events, 0.0 us)
Async XLA Ops:
  8.5 2.6 %copy-start = (bf16[2,64,4096]{2,1,0:T(8,128)(2,1)S(1)}, bf16[2,64,4096]{2,1,0:T(8,128)(2,1)}, u32[]{:S(2)}) copy-start(bf16[2,64,4096]{2,1,0:T(8,128)(2,1)} %param.14) | copy-start | bytes 3145732
  8.5 2.6 %copy-start.1 = (f32[9,2048]{1,0:T(8,128)S(1)}, f32[9,2048]{1,0:T(8,128)}, u32[]{:S(2)}) copy-start(f32[9,2048]{1,0:T(8,128)} %constant.57.clone.sin_t) | copy-start | bytes 221188
  8.6 2.6 %copy-start.2 = (f32[9,2048]{1,0:T(8,128)S(1)}, f32[9,2048]{1,0:T(8,128)}, u32[]{:S(2)}) copy-start(f32[9,2048]{1,0:T(8,128)} %constant.56.clone.cos_t) | copy-start | bytes 221188
  8.6 2.6 %copy-start.3 = (f32[128,128]{1,0:T(8,128)S(1)}, f32[128,128]{1,0:T(8,128)}, u32[]{:S(2)}) copy-start(f32[128,128]{1,0:T(8,128)} %constant.58.clone.cols) | copy-start | bytes 196612
  8.6 2.5 %copy-start.4 = (f32[2048]{0:T(1024)S(1)}, f32[2048]{0:T(1024)}, u32[]{:S(2)}) copy-start(f32[2048]{0:T(1024)} %param.15) | copy-start | bytes 24580
  8.6 2.5 %copy-start.5 = (f32[2]{0:T(128)S(1)}, f32[2]{0:T(128)}, u32[]{:S(2)}) copy-start(f32[2]{0:T(128)} %bias.1) | copy-start | bytes 28
